TPU v7x, 32 devices: a whole 2x2x4 slice. The times are simulated.
32 devices in a mesh: groups: 2 (over y), tm: 4 (over z), section: 2 (over x), head: 2 (over core).
Axes of the slice: x: 2, y: 2, z: 4, core: 2. Of those that a mesh axis runs over, the one named last changes fastest.
Arguments:
- latent: bfloat16 [4, 128, 5120], P(('groups', 'section'), 'tm', 'head'), parts along dimension 0, may hold values from -6 to 6
- head_weights: bfloat16 [2, 4, 40, 128, 128], P('section', None, 'head')
- modulation: float32 [2, 3, 5120], P('section', None, 'head'), may hold values from -3 to 3
- tile_mask: int32 [8, 2, 6], P(('groups', 'tm')), parts along dimension 0, may hold values from 0 to 1
- window: int32 [4], P('groups'), parts along dimension 0, may hold values from 1 to 3, as said below
Outputs:
- denoised: bfloat16 [4, 128, 5120], P(('groups', 'section'), 'tm', 'head'), parts along dimension 0
There are 2 independent parts, one for each index of `groups`. A program takes and returns all parts, laid end to end along the dimension named above; an argument that names none is the same for every part. Nothing has to cross between parts.
Inputs may be any that keep to these rules, and one draw needn't show every extreme that they name: Some clip has a window of exactly 3 stretches.
All inputs are finite; a program needn't handle non-finite values.
Results may differ from a plain program's by a relative error of at most 0.0055.
Values may be sent and summed in bfloat16 or wider, within the bound.
A program may use at most 64 MiB of HBM per device.

v0:
```python
import math

import jax
import jax.numpy as jnp
from jax import lax
from jax.sharding import PartitionSpec as P

D = 5120


epsilon = 1e-06


def from_behind(block, axis, distance):
    devices = range(lax.axis_size(axis))
    route = [(i - distance, i) for i in devices if i - distance in devices]
    return lax.ppermute(block, axis, route)


def passed_along(block, axis, distance):
    devices = range(lax.axis_size(axis))
    route = [((i - distance) % len(devices), i) for i in devices]
    return lax.ppermute(block, axis, route)


def shards(latent, head_weights, modulation, tile_mask, window):
    section_count = lax.axis_size("section")
    my_section = lax.axis_index("section")
    my_stretch = lax.axis_index("tm")
    row_count = latent.shape[1]
    feature_count = latent.shape[2]
    weights = head_weights[0]
    head_count = weights.shape[1]
    head_size = weights.shape[2]
    modulate = modulation[0]
    tile_marks = tile_mask[0]
    tile_count = tile_marks.shape[0]
    span_count = tile_marks.shape[1] // tile_count
    tile_rows = row_count // tile_count
    scale_factor = 1.0 / math.sqrt(head_size)
    expanded = jnp.repeat(jnp.repeat(tile_marks, tile_rows, axis=0), tile_rows, axis=1) == 1
    query_tile = jnp.arange(row_count) // tile_rows
    key_index = jnp.arange(span_count * row_count)
    key_dist = span_count - 1 - key_index // row_count
    key_tile = key_index % row_count // tile_rows
    own_tile = (key_dist == 0)[None, :] & (query_tile[:, None] == key_tile[None, :])
    fixed_mask = expanded | own_tile
    reachable = my_stretch - key_dist >= 0

    def tick_body(tick_index, current):
        clip_index = (my_section - tick_index) % section_count
        active = tick_index == my_section + (section_count - clip_index) % section_count
        win_len = window[clip_index]
        allowed = fixed_mask & (reachable & (key_dist < win_len))[None, :]
        values = current.astype(jnp.float32)
        square_sum = lax.psum(jnp.sum(values * values, axis=-1), "head")
        mean_sq = (square_sum / D)[:, None]
        normed = (values * lax.rsqrt(mean_sq + epsilon) * (1.0 + modulate[1]) + modulate[0]).astype(
            jnp.bfloat16
        )
        heads_in = normed.reshape(row_count, head_count, head_size)
        projected = jnp.einsum(
            "rhd,mhde->mrhe", heads_in, weights[:3], preferred_element_type=jnp.float32
        ).astype(jnp.bfloat16)
        key_value = projected[1:].reshape(2, row_count, feature_count)
        earlier = []
        passed = key_value
        for offset in range(1, span_count):
            passed = from_behind(passed, "tm", 1)
            earlier.append(passed)
        window_keys = jnp.concatenate(earlier[::-1] + [key_value], axis=1)
        window_keys = window_keys.reshape(2, span_count * row_count, head_count, head_size)
        scores = (
            jnp.einsum(
                "qhd,khd->hqk", projected[0], window_keys[0], preferred_element_type=jnp.float32
            )
            * scale_factor
        )
        scores = jnp.where(allowed[None], scores, -1e30)
        row_peak = jnp.max(scores, axis=-1, keepdims=True)
        exponentials = jnp.exp(scores - row_peak)
        attn_probs = (exponentials / jnp.sum(exponentials, axis=-1, keepdims=True)).astype(
            jnp.bfloat16
        )
        attended = jnp.einsum(
            "hqk,khd->qhd", attn_probs, window_keys[1], preferred_element_type=jnp.float32
        ).astype(jnp.bfloat16)
        mixed_out = jnp.einsum(
            "qhd,hde->qhe", attended, weights[3], preferred_element_type=jnp.float32
        ).reshape(row_count, feature_count)
        updated = (values + modulate[2] * mixed_out).astype(jnp.bfloat16)
        current = jnp.where(active, updated, current)
        return passed_along(current, "section", 1)

    finished = lax.fori_loop(0, 2 * section_count, tick_body, latent[0])
    return finished[None]


def solution(mesh):
    return jax.shard_map(
        shards,
        mesh=mesh,
        in_specs=(
            P(("groups", "section"), "tm", "head"),
            P("section", None, "head", None, None),
            P("section", None, "head"),
            P(("groups", "tm"), None, None),
            P("groups"),
        ),
        out_specs=P(("groups", "section"), "tm", "head"),
        check_vma=False,
    )
```

profile of v0, /device:TPU:2, one launch (start us, length us, event | category | flops | bytes accessed | tf_op | source)
XLA Modules:
  0.0 178.8 jit_solution(13995954548523162741)
XLA Ops:
  3.3 174.9 %while.16 = (s32[]{:T(128)}, bf16[32,2560]{1,0:T(8,128)(2,1)S(1)}, s32[]{:T(128)}, f32[3,2560]{1,0:T(4,128)S(1)}, bf16[4,20,128,128]{3,2,0,1:T(8,128)(2,1)S(1)},...) while((s32[]{:T(128)}, bf16[32,2560]{1,0:T(8,128)(2,1)S(1)}, ...), condition=%wide.region_5.6_spmd.clone, body=%wide.region_0.5_spmd.clone.sunk | while | flops 117183072 | bytes 18446128 | solution.py:95
  3.5 2.5 %psum.16 = f32[32]{0:T(128)S(1)} all-reduce(f32[32]{0:T(128)S(1)} %fusion.62), channel_id=1, replica_groups=mesh['groups'=2,'tm'=4,'section'=2,'head'=2] {'head'}, use_global_device_ids=true, to_apply=%region_2.2 | all-reduce | flops 32 | bytes 256 | tf_op jit(solution)/shard_map/while/body/eval_jaxpr/psum | solution.py:56
  7.4 4.2 %collective-permute-start = (bf16[2,32,2560]{2,1,0:T(8,128)(2,1)}, bf16[2,32,2560]{2,1,0:T(8,128)(2,1)}, u32[]{:S(2)}, u32[]{:S(2)}) collective-permute-start(bf16[2,32,2560]{2,1,0:T(8,128)(2,1)} %copy_bitcast_fusion.4), channel_id=1, source_target_pairs={{0,4},{4,8},{8,12},{1,5},{5,9},{9,13},{2,6},{6,10},{10,14},{3,7},{... | collective-permute-start | bytes 983048 | tf_op jit(solution)/shard_map/while/body/eval_jaxpr/ppermute | solution.py:17
  12.3 6.2 %collective-permute-done = bf16[2,32,2560]{2,1,0:T(8,128)(2,1)} collective-permute-done((bf16[2,32,2560]{2,1,0:T(8,128)(2,1)}, bf16[2,32,2560]{2,1,0:T(8,128)(2,1)}, u32[]{:S(2)}, u32[]{:S(2)}) %collective-permute-start) | collective-permute-done | bytes 327712 | tf_op jit(solution)/shard_map/while/body/eval_jaxpr/ppermute | solution.py:17
  18.5 4.4 %collective-permute-start.1 = (bf16[2,32,2560]{2,1,0:T(8,128)(2,1)}, bf16[2,32,2560]{2,1,0:T(8,128)(2,1)S(1)}, u32[]{:S(2)}, u32[]{:S(2)}) collective-permute-start(bf16[2,32,2560]{2,1,0:T(8,128)(2,1)} %collective-permute-done), channel_id=1, source_target_pairs={{0,4},{4,8},{8,12},{1,5},{5,9},{9,13},{2,6},{6,10},{10,14},{3,7},{... | collective-permute-start | bytes 983048 | tf_op jit(solution)/shard_map/while/body/eval_jaxpr/ppermute | solution.py:17
  23.6 6.0 %collective-permute-done.1 = bf16[2,32,2560]{2,1,0:T(8,128)(2,1)S(1)} collective-permute-done((bf16[2,32,2560]{2,1,0:T(8,128)(2,1)}, bf16[2,32,2560]{2,1,0:T(8,128)(2,1)S(1)}, u32[]{:S(2)}, u32[]{:S(2)}) %collective-permute-start.1) | collective-permute-done | bytes 327712 | tf_op jit(solution)/shard_map/while/body/eval_jaxpr/ppermute | solution.py:17
  33.9 2.1 %squeeze.74 = bf16[96,20,128]{2,1,0:T(8,128)(2,1)} reshape(bf16[1,96,2560]{2,1,0:T(8,128)(2,1)} %get-tuple-element.360) | data formatting | bytes 983040 | tf_op jit(solution)/shard_map/while/body/eval_jaxpr/squeeze | solution.py:75
  38.5 2.5 %convolution_bitcast_fusion.2 = f32[20,4,8,128]{3,2,1,0:T(8,128)S(1)} fusion(bf16[96,20,128]{2,1,0:T(8,128)(2,1)} %squeeze.73, f32[20,32]{1,0:T(8,128)S(1)} %fusion.67, f32[20,32,96]{2,1,0:T(8,128)} %copy-done.1, bf16[4,20,128,128]{3,2,0,1:T(8,128)(2,1)S(1)} %get-tuple-element.394), kind=kOutput, calls=%fused_computation.9.clone.1 | convolution fusion | flops 36967136 | bytes 2240512 | tf_op jit(solution)/shard_map/while/body/eval_jaxpr/qhd,hde->qhe/dot_general | solution.py:88
  41.6 4.8 %collective-permute-done.2 = bf16[32,2560]{1,0:T(8,128)(2,1)S(1)} collective-permute-done((bf16[32,2560]{1,0:T(8,128)(2,1)S(1)}, bf16[32,2560]{1,0:T(8,128)(2,1)S(1)}, u32[]{:S(2)}, u32[]{:S(2)}) %collective-permute-start.2) | collective-permute-done | bytes 163872 | tf_op jit(solution)/shard_map/while/body/eval_jaxpr/ppermute | solution.py:23
  46.6 2.5 %psum.16 = f32[32]{0:T(128)S(1)} all-reduce(f32[32]{0:T(128)S(1)} %fusion.62), channel_id=1, replica_groups=mesh['groups'=2,'tm'=4,'section'=2,'head'=2] {'head'}, use_global_device_ids=true, to_apply=%region_2.2 | all-reduce | flops 32 | bytes 256 | tf_op jit(solution)/shard_map/while/body/eval_jaxpr/psum | solution.py:56
  50.6 5.0 %collective-permute-start = (bf16[2,32,2560]{2,1,0:T(8,128)(2,1)}, bf16[2,32,2560]{2,1,0:T(8,128)(2,1)}, u32[]{:S(2)}, u32[]{:S(2)}) collective-permute-start(bf16[2,32,2560]{2,1,0:T(8,128)(2,1)} %copy_bitcast_fusion.4), channel_id=1, source_target_pairs={{0,4},{4,8},{8,12},{1,5},{5,9},{9,13},{2,6},{6,10},{10,14},{3,7},{... | collective-permute-start | bytes 983048 | tf_op jit(solution)/shard_map/while/body/eval_jaxpr/ppermute | solution.py:17
  56.2 6.2 %collective-permute-done = bf16[2,32,2560]{2,1,0:T(8,128)(2,1)} collective-permute-done((bf16[2,32,2560]{2,1,0:T(8,128)(2,1)}, bf16[2,32,2560]{2,1,0:T(8,128)(2,1)}, u32[]{:S(2)}, u32[]{:S(2)}) %collective-permute-start) | collective-permute-done | bytes 327712 | tf_op jit(solution)/shard_map/while/body/eval_jaxpr/ppermute | solution.py:17
  62.4 4.4 %collective-permute-start.1 = (bf16[2,32,2560]{2,1,0:T(8,128)(2,1)}, bf16[2,32,2560]{2,1,0:T(8,128)(2,1)S(1)}, u32[]{:S(2)}, u32[]{:S(2)}) collective-permute-start(bf16[2,32,2560]{2,1,0:T(8,128)(2,1)} %collective-permute-done), channel_id=1, source_target_pairs={{0,4},{4,8},{8,12},{1,5},{5,9},{9,13},{2,6},{6,10},{10,14},{3,7},{... | collective-permute-start | bytes 983048 | tf_op jit(solution)/shard_map/while/body/eval_jaxpr/ppermute | solution.py:17
  67.6 6.0 %collective-permute-done.1 = bf16[2,32,2560]{2,1,0:T(8,128)(2,1)S(1)} collective-permute-done((bf16[2,32,2560]{2,1,0:T(8,128)(2,1)}, bf16[2,32,2560]{2,1,0:T(8,128)(2,1)S(1)}, u32[]{:S(2)}, u32[]{:S(2)}) %collective-permute-start.1) | collective-permute-done | bytes 327712 | tf_op jit(solution)/shard_map/while/body/eval_jaxpr/ppermute | solution.py:17
  77.8 2.1 %squeeze.74 = bf16[96,20,128]{2,1,0:T(8,128)(2,1)} reshape(bf16[1,96,2560]{2,1,0:T(8,128)(2,1)} %get-tuple-element.360) | data formatting | bytes 983040 | tf_op jit(solution)/shard_map/while/body/eval_jaxpr/squeeze | solution.py:75
  82.4 2.5 %convolution_bitcast_fusion.2 = f32[20,4,8,128]{3,2,1,0:T(8,128)S(1)} fusion(bf16[96,20,128]{2,1,0:T(8,128)(2,1)} %squeeze.73, f32[20,32]{1,0:T(8,128)S(1)} %fusion.67, f32[20,32,96]{2,1,0:T(8,128)} %copy-done.1, bf16[4,20,128,128]{3,2,0,1:T(8,128)(2,1)S(1)} %get-tuple-element.394), kind=kOutput, calls=%fused_computation.9.clone.1 | convolution fusion | flops 36967136 | bytes 2240512 | tf_op jit(solution)/shard_map/while/body/eval_jaxpr/qhd,hde->qhe/dot_general | solution.py:88
  85.5 4.8 %collective-permute-done.2 = bf16[32,2560]{1,0:T(8,128)(2,1)S(1)} collective-permute-done((bf16[32,2560]{1,0:T(8,128)(2,1)S(1)}, bf16[32,2560]{1,0:T(8,128)(2,1)S(1)}, u32[]{:S(2)}, u32[]{:S(2)}) %collective-permute-start.2) | collective-permute-done | bytes 163872 | tf_op jit(solution)/shard_map/while/body/eval_jaxpr/ppermute | solution.py:23
  90.5 2.5 %psum.16 = f32[32]{0:T(128)S(1)} all-reduce(f32[32]{0:T(128)S(1)} %fusion.62), channel_id=1, replica_groups=mesh['groups'=2,'tm'=4,'section'=2,'head'=2] {'head'}, use_global_device_ids=true, to_apply=%region_2.2 | all-reduce | flops 32 | bytes 256 | tf_op jit(solution)/shard_map/while/body/eval_jaxpr/psum | solution.py:56
  94.5 5.0 %collective-permute-start = (bf16[2,32,2560]{2,1,0:T(8,128)(2,1)}, bf16[2,32,2560]{2,1,0:T(8,128)(2,1)}, u32[]{:S(2)}, u32[]{:S(2)}) collective-permute-start(bf16[2,32,2560]{2,1,0:T(8,128)(2,1)} %copy_bitcast_fusion.4), channel_id=1, source_target_pairs={{0,4},{4,8},{8,12},{1,5},{5,9},{9,13},{2,6},{6,10},{10,14},{3,7},{... | collective-permute-start | bytes 983048 | tf_op jit(solution)/shard_map/while/body/eval_jaxpr/ppermute | solution.py:17
  100.2 6.2 %collective-permute-done = bf16[2,32,2560]{2,1,0:T(8,128)(2,1)} collective-permute-done((bf16[2,32,2560]{2,1,0:T(8,128)(2,1)}, bf16[2,32,2560]{2,1,0:T(8,128)(2,1)}, u32[]{:S(2)}, u32[]{:S(2)}) %collective-permute-start) | collective-permute-done | bytes 327712 | tf_op jit(solution)/shard_map/while/body/eval_jaxpr/ppermute | solution.py:17
  106.4 4.4 %collective-permute-start.1 = (bf16[2,32,2560]{2,1,0:T(8,128)(2,1)}, bf16[2,32,2560]{2,1,0:T(8,128)(2,1)S(1)}, u32[]{:S(2)}, u32[]{:S(2)}) collective-permute-start(bf16[2,32,2560]{2,1,0:T(8,128)(2,1)} %collective-permute-done), channel_id=1, source_target_pairs={{0,4},{4,8},{8,12},{1,5},{5,9},{9,13},{2,6},{6,10},{10,14},{3,7},{... | collective-permute-start | bytes 983048 | tf_op jit(solution)/shard_map/while/body/eval_jaxpr/ppermute | solution.py:17
  111.5 6.0 %collective-permute-done.1 = bf16[2,32,2560]{2,1,0:T(8,128)(2,1)S(1)} collective-permute-done((bf16[2,32,2560]{2,1,0:T(8,128)(2,1)}, bf16[2,32,2560]{2,1,0:T(8,128)(2,1)S(1)}, u32[]{:S(2)}, u32[]{:S(2)}) %collective-permute-start.1) | collective-permute-done | bytes 327712 | tf_op jit(solution)/shard_map/while/body/eval_jaxpr/ppermute | solution.py:17
  121.7 2.1 %squeeze.74 = bf16[96,20,128]{2,1,0:T(8,128)(2,1)} reshape(bf16[1,96,2560]{2,1,0:T(8,128)(2,1)} %get-tuple-element.360) | data formatting | bytes 983040 | tf_op jit(solution)/shard_map/while/body/eval_jaxpr/squeeze | solution.py:75
  126.3 2.5 %convolution_bitcast_fusion.2 = f32[20,4,8,128]{3,2,1,0:T(8,128)S(1)} fusion(bf16[96,20,128]{2,1,0:T(8,128)(2,1)} %squeeze.73, f32[20,32]{1,0:T(8,128)S(1)} %fusion.67, f32[20,32,96]{2,1,0:T(8,128)} %copy-done.1, bf16[4,20,128,128]{3,2,0,1:T(8,128)(2,1)S(1)} %get-tuple-element.394), kind=kOutput, calls=%fused_computation.9.clone.1 | convolution fusion | flops 36967136 | bytes 2240512 | tf_op jit(solution)/shard_map/while/body/eval_jaxpr/qhd,hde->qhe/dot_general | solution.py:88
  129.4 4.8 %collective-permute-done.2 = bf16[32,2560]{1,0:T(8,128)(2,1)S(1)} collective-permute-done((bf16[32,2560]{1,0:T(8,128)(2,1)S(1)}, bf16[32,2560]{1,0:T(8,128)(2,1)S(1)}, u32[]{:S(2)}, u32[]{:S(2)}) %collective-permute-start.2) | collective-permute-done | bytes 163872 | tf_op jit(solution)/shard_map/while/body/eval_jaxpr/ppermute | solution.py:23
  134.5 2.5 %psum.16 = f32[32]{0:T(128)S(1)} all-reduce(f32[32]{0:T(128)S(1)} %fusion.62), channel_id=1, replica_groups=mesh['groups'=2,'tm'=4,'section'=2,'head'=2] {'head'}, use_global_device_ids=true, to_apply=%region_2.2 | all-reduce | flops 32 | bytes 256 | tf_op jit(solution)/shard_map/while/body/eval_jaxpr/psum | solution.py:56
  138.4 5.0 %collective-permute-start = (bf16[2,32,2560]{2,1,0:T(8,128)(2,1)}, bf16[2,32,2560]{2,1,0:T(8,128)(2,1)}, u32[]{:S(2)}, u32[]{:S(2)}) collective-permute-start(bf16[2,32,2560]{2,1,0:T(8,128)(2,1)} %copy_bitcast_fusion.4), channel_id=1, source_target_pairs={{0,4},{4,8},{8,12},{1,5},{5,9},{9,13},{2,6},{6,10},{10,14},{3,7},{... | collective-permute-start | bytes 983048 | tf_op jit(solution)/shard_map/while/body/eval_jaxpr/ppermute | solution.py:17
  144.1 6.2 %collective-permute-done = bf16[2,32,2560]{2,1,0:T(8,128)(2,1)} collective-permute-done((bf16[2,32,2560]{2,1,0:T(8,128)(2,1)}, bf16[2,32,2560]{2,1,0:T(8,128)(2,1)}, u32[]{:S(2)}, u32[]{:S(2)}) %collective-permute-start) | collective-permute-done | bytes 327712 | tf_op jit(solution)/shard_map/while/body/eval_jaxpr/ppermute | solution.py:17
  150.3 4.4 %collective-permute-start.1 = (bf16[2,32,2560]{2,1,0:T(8,128)(2,1)}, bf16[2,32,2560]{2,1,0:T(8,128)(2,1)S(1)}, u32[]{:S(2)}, u32[]{:S(2)}) collective-permute-start(bf16[2,32,2560]{2,1,0:T(8,128)(2,1)} %collective-permute-done), channel_id=1, source_target_pairs={{0,4},{4,8},{8,12},{1,5},{5,9},{9,13},{2,6},{6,10},{10,14},{3,7},{... | collective-permute-start | bytes 983048 | tf_op jit(solution)/shard_map/while/body/eval_jaxpr/ppermute | solution.py:17
  155.4 6.0 %collective-permute-done.1 = bf16[2,32,2560]{2,1,0:T(8,128)(2,1)S(1)} collective-permute-done((bf16[2,32,2560]{2,1,0:T(8,128)(2,1)}, bf16[2,32,2560]{2,1,0:T(8,128)(2,1)S(1)}, u32[]{:S(2)}, u32[]{:S(2)}) %collective-permute-start.1) | collective-permute-done | bytes 327712 | tf_op jit(solution)/shard_map/while/body/eval_jaxpr/ppermute | solution.py:17
  170.2 2.5 %convolution_bitcast_fusion.2 = f32[20,4,8,128]{3,2,1,0:T(8,128)S(1)} fusion(bf16[96,20,128]{2,1,0:T(8,128)(2,1)} %squeeze.73, f32[20,32]{1,0:T(8,128)S(1)} %fusion.67, f32[20,32,96]{2,1,0:T(8,128)} %copy-done.1, bf16[4,20,128,128]{3,2,0,1:T(8,128)(2,1)S(1)} %get-tuple-element.394), kind=kOutput, calls=%fused_computation.9.clone.1 | convolution fusion | flops 36967136 | bytes 2240512 | tf_op jit(solution)/shard_map/while/body/eval_jaxpr/qhd,hde->qhe/dot_general | solution.py:88
  173.4 4.8 %collective-permute-done.2 = bf16[32,2560]{1,0:T(8,128)(2,1)S(1)} collective-permute-done((bf16[32,2560]{1,0:T(8,128)(2,1)S(1)}, bf16[32,2560]{1,0:T(8,128)(2,1)S(1)}, u32[]{:S(2)}, u32[]{:S(2)}) %collective-permute-start.2) | collective-permute-done | bytes 163872 | tf_op jit(solution)/shard_map/while/body/eval_jaxpr/ppermute | solution.py:23
  (109 shorter events, 47.4 us)
Async XLA Ops:
  0.8 2.1 %copy-start.2 = (s32[1,2,6]{2,1,0:T(2,128)S(1)}, s32[1,2,6]{2,1,0:T(2,128)}, u32[]{:S(2)}) copy-start(s32[1,2,6]{2,1,0:T(2,128)} %param.10) | copy-start | bytes 148
  0.8 2.5 %copy-start = (bf16[1,32,2560]{2,1,0:T(8,128)(2,1)S(1)}, bf16[1,32,2560]{2,1,0:T(8,128)(2,1)}, u32[]{:S(2)}) copy-start(bf16[1,32,2560]{2,1,0:T(8,128)(2,1)} %param.7) | copy-start | bytes 491524
  0.8 2.5 %copy-start.3 = (s32[2]{0:T(128)S(1)}, s32[2]{0:T(128)}, u32[]{:S(2)}) copy-start(s32[2]{0:T(128)} %param.11) | copy-start | bytes 28
  7.4 11.1 %collective-permute-start = (bf16[2,32,2560]{2,1,0:T(8,128)(2,1)}, bf16[2,32,2560]{2,1,0:T(8,128)(2,1)}, u32[]{:S(2)}, u32[]{:S(2)}) collective-permute-start(bf16[2,32,2560]{2,1,0:T(8,128)(2,1)} %copy_bitcast_fusion.4), channel_id=1, source_target_pairs={{0,4},{4,8},{8,12},{1,5},{5,9},{9,13},{2,6},{6,10},{10,14},{3,7},{... | collective-permute-start | bytes 983048 | tf_op jit(solution)/shard_map/while/body/eval_jaxpr/ppermute | solution.py:17
  18.5 11.1 %collective-permute-start.1 = (bf16[2,32,2560]{2,1,0:T(8,128)(2,1)}, bf16[2,32,2560]{2,1,0:T(8,128)(2,1)S(1)}, u32[]{:S(2)}, u32[]{:S(2)}) collective-permute-start(bf16[2,32,2560]{2,1,0:T(8,128)(2,1)} %collective-permute-done), channel_id=1, source_target_pairs={{0,4},{4,8},{8,12},{1,5},{5,9},{9,13},{2,6},{6,10},{10,14},{3,7},{... | collective-permute-start | bytes 983048 | tf_op jit(solution)/shard_map/while/body/eval_jaxpr/ppermute | solution.py:17
  37.5 0.7 copy-start.1
  41.0 5.4 %collective-permute-start.2 = (bf16[32,2560]{1,0:T(8,128)(2,1)S(1)}, bf16[32,2560]{1,0:T(8,128)(2,1)S(1)}, u32[]{:S(2)}, u32[]{:S(2)}) collective-permute-start(bf16[32,2560]{1,0:T(8,128)(2,1)S(1)} %fusion.68), channel_id=1, source_target_pairs={{2,0},{0,2},{3,1},{1,3},{6,4},{4,6},{7,5},{5,7},{10,8},{8,10},{11,... | collective-permute-start | bytes 491528 | tf_op jit(solution)/shard_map/while/body/eval_jaxpr/ppermute | solution.py:23
  50.6 11.9 %collective-permute-start = (bf16[2,32,2560]{2,1,0:T(8,128)(2,1)}, bf16[2,32,2560]{2,1,0:T(8,128)(2,1)}, u32[]{:S(2)}, u32[]{:S(2)}) collective-permute-start(bf16[2,32,2560]{2,1,0:T(8,128)(2,1)} %copy_bitcast_fusion.4), channel_id=1, source_target_pairs={{0,4},{4,8},{8,12},{1,5},{5,9},{9,13},{2,6},{6,10},{10,14},{3,7},{... | collective-permute-start | bytes 983048 | tf_op jit(solution)/shard_map/while/body/eval_jaxpr/ppermute | solution.py:17
  62.4 11.1 %collective-permute-start.1 = (bf16[2,32,2560]{2,1,0:T(8,128)(2,1)}, bf16[2,32,2560]{2,1,0:T(8,128)(2,1)S(1)}, u32[]{:S(2)}, u32[]{:S(2)}) collective-permute-start(bf16[2,32,2560]{2,1,0:T(8,128)(2,1)} %collective-permute-done), channel_id=1, source_target_pairs={{0,4},{4,8},{8,12},{1,5},{5,9},{9,13},{2,6},{6,10},{10,14},{3,7},{... | collective-permute-start | bytes 983048 | tf_op jit(solution)/shard_map/while/body/eval_jaxpr/ppermute | solution.py:17
  81.4 0.7 copy-start.1
  84.9 5.4 %collective-permute-start.2 = (bf16[32,2560]{1,0:T(8,128)(2,1)S(1)}, bf16[32,2560]{1,0:T(8,128)(2,1)S(1)}, u32[]{:S(2)}, u32[]{:S(2)}) collective-permute-start(bf16[32,2560]{1,0:T(8,128)(2,1)S(1)} %fusion.68), channel_id=1, source_target_pairs={{2,0},{0,2},{3,1},{1,3},{6,4},{4,6},{7,5},{5,7},{10,8},{8,10},{11,... | collective-permute-start | bytes 491528 | tf_op jit(solution)/shard_map/while/body/eval_jaxpr/ppermute | solution.py:23
  94.5 11.9 %collective-permute-start = (bf16[2,32,2560]{2,1,0:T(8,128)(2,1)}, bf16[2,32,2560]{2,1,0:T(8,128)(2,1)}, u32[]{:S(2)}, u32[]{:S(2)}) collective-permute-start(bf16[2,32,2560]{2,1,0:T(8,128)(2,1)} %copy_bitcast_fusion.4), channel_id=1, source_target_pairs={{0,4},{4,8},{8,12},{1,5},{5,9},{9,13},{2,6},{6,10},{10,14},{3,7},{... | collective-permute-start | bytes 983048 | tf_op jit(solution)/shard_map/while/body/eval_jaxpr/ppermute | solution.py:17
  106.4 11.1 %collective-permute-start.1 = (bf16[2,32,2560]{2,1,0:T(8,128)(2,1)}, bf16[2,32,2560]{2,1,0:T(8,128)(2,1)S(1)}, u32[]{:S(2)}, u32[]{:S(2)}) collective-permute-start(bf16[2,32,2560]{2,1,0:T(8,128)(2,1)} %collective-permute-done), channel_id=1, source_target_pairs={{0,4},{4,8},{8,12},{1,5},{5,9},{9,13},{2,6},{6,10},{10,14},{3,7},{... | collective-permute-start | bytes 983048 | tf_op jit(solution)/shard_map/while/body/eval_jaxpr/ppermute | solution.py:17
  125.3 0.7 copy-start.1
  128.8 5.4 %collective-permute-start.2 = (bf16[32,2560]{1,0:T(8,128)(2,1)S(1)}, bf16[32,2560]{1,0:T(8,128)(2,1)S(1)}, u32[]{:S(2)}, u32[]{:S(2)}) collective-permute-start(bf16[32,2560]{1,0:T(8,128)(2,1)S(1)} %fusion.68), channel_id=1, source_target_pairs={{2,0},{0,2},{3,1},{1,3},{6,4},{4,6},{7,5},{5,7},{10,8},{8,10},{11,... | collective-permute-start | bytes 491528 | tf_op jit(solution)/shard_map/while/body/eval_jaxpr/ppermute | solution.py:23
  138.4 11.9 %collective-permute-start = (bf16[2,32,2560]{2,1,0:T(8,128)(2,1)}, bf16[2,32,2560]{2,1,0:T(8,128)(2,1)}, u32[]{:S(2)}, u32[]{:S(2)}) collective-permute-start(bf16[2,32,2560]{2,1,0:T(8,128)(2,1)} %copy_bitcast_fusion.4), channel_id=1, source_target_pairs={{0,4},{4,8},{8,12},{1,5},{5,9},{9,13},{2,6},{6,10},{10,14},{3,7},{... | collective-permute-start | bytes 983048 | tf_op jit(solution)/shard_map/while/body/eval_jaxpr/ppermute | solution.py:17
  150.3 11.1 %collective-permute-start.1 = (bf16[2,32,2560]{2,1,0:T(8,128)(2,1)}, bf16[2,32,2560]{2,1,0:T(8,128)(2,1)S(1)}, u32[]{:S(2)}, u32[]{:S(2)}) collective-permute-start(bf16[2,32,2560]{2,1,0:T(8,128)(2,1)} %collective-permute-done), channel_id=1, source_target_pairs={{0,4},{4,8},{8,12},{1,5},{5,9},{9,13},{2,6},{6,10},{10,14},{3,7},{... | collective-permute-start | bytes 983048 | tf_op jit(solution)/shard_map/while/body/eval_jaxpr/ppermute | solution.py:17
  169.2 0.7 copy-start.1
  172.8 5.4 %collective-permute-start.2 = (bf16[32,2560]{1,0:T(8,128)(2,1)S(1)}, bf16[32,2560]{1,0:T(8,128)(2,1)S(1)}, u32[]{:S(2)}, u32[]{:S(2)}) collective-permute-start(bf16[32,2560]{1,0:T(8,128)(2,1)S(1)} %fusion.68), channel_id=1, source_target_pairs={{2,0},{0,2},{3,1},{1,3},{6,4},{4,6},{7,5},{5,7},{10,8},{8,10},{11,... | collective-permute-start | bytes 491528 | tf_op jit(solution)/shard_map/while/body/eval_jaxpr/ppermute | solution.py:23
where the time goes:
time: 182 us; the launch traced here: 179 us
  waiting for transfers between devices  68 us (37%)
  starting transfers between devices  39.1 us (21%)
  local copies, waits for them, and re-layouts  38.4 us (21%)
  matrix products  17.4 us (10%)
  blocking collectives  9.85 us (5%)
  other arithmetic  5.56 us (3%)
    ppermute x8, waiting for transfers between devices, from_behind(): return lax.ppermute(block, axis, route)  48.9 us
    ppermute x8, starting transfers between devices, from_behind(): return lax.ppermute(block, axis, route)  36.7 us
    ppermute x4, waiting for transfers between devices, passed_along(): return lax.ppermute(block, axis, route)  19.1 us
    dot_general x4, matrix products, tick_body(): jnp.einsum('qhd,hde->qhe', attended, weights[3], preferred_element_type=j...  9.87 us
    psum x4, blocking collectives, tick_body(): square_sum = lax.psum(jnp.sum(values * values, axis=-1), 'head')  9.85 us
    squeeze x4, local copies, waits for them, and re-layouts, tick_body(): window_keys[0]  8.57 us
    squeeze x4, local copies, waits for them, and re-layouts, tick_body(): window_keys[1]  8.56 us
    while x16, local copies, waits for them, and re-layouts  7.01 us
  transfers between devices with their start and end apart: 12, of which 12 were waited for; matrix products, arithmetic and copies ran while one was open for 3% of the time, Pallas kernels for 0%

commit v1 on v0

--- a/solution.py
+++ b/solution.py
@@ -1,14 +1,18 @@
+import functools
 import math
 
 import jax
 import jax.numpy as jnp
 from jax import lax
+from jax.experimental import pallas as pl
+from jax.experimental.pallas import tpu as pltpu
 from jax.sharding import PartitionSpec as P
 
 D = 5120
 
 
 epsilon = 1e-06
+MESH_IDS = pl.DeviceIdType.MESH
 
 
 def from_behind(block, axis, distance):
@@ -23,7 +27,7 @@
     return lax.ppermute(block, axis, route)
 
 
-def shards(latent, head_weights, modulation, tile_mask, window):
+def ring_shards(latent, head_weights, modulation, tile_mask, window):
     section_count = lax.axis_size("section")
     my_section = lax.axis_index("section")
     my_stretch = lax.axis_index("tm")
@@ -96,7 +100,316 @@
     return finished[None]
 
 
+def rollout_kernel(
+    stretches, cores,
+    marks_ref, window_ref, latent_ref, weights_ref, modulation_ref,
+    out_ref,
+    xin, xmid, stage, marks, held, mods, squares,
+    in_send, in_recv, mark_send, mark_recv, own_sem, mod_sem, modx_sem,
+    local_sem, x_send, x_recv, y_send, y_recv,
+    sq_send, sq_recv, out_send, out_recv, out_own,
+):
+    g = lax.axis_index("groups")
+    t = lax.axis_index("tm")
+    s = lax.axis_index("section")
+    h = lax.axis_index("head")
+    heads = held.shape[2]
+    size = held.shape[3]
+    rows = xin.shape[1]
+    width = heads * size
+    tokens = stretches * rows
+    tiles = marks_ref.shape[1]
+    columns = marks_ref.shape[2]
+    span = columns // tiles
+    scale = 1.0 / math.sqrt(size)
+    other_s = 1 - s
+    other_g = 1 - g
+
+    peers = [
+        (dt, dh, lax.rem(t + dt, stretches), lax.rem(h + dh, cores))
+        for dt in range(stretches) for dh in range(cores) if (dt, dh) != (0, 0)
+    ]
+
+    def lanes(stretch):
+        return pl.ds(pl.multiple_of(stretch * width, size), width)
+
+    def remote(src, dst, send, recv, **where):
+        return pltpu.make_async_remote_copy(
+            src_ref=src, dst_ref=dst, send_sem=send, recv_sem=recv,
+            device_id=where, device_id_type=MESH_IDS,
+        )
+
+    barrier = pltpu.get_barrier_semaphore()
+    for dt, dh, pt, ph in peers:
+        pl.semaphore_signal(barrier, inc=1, device_id={"tm": pt, "head": ph}, device_id_type=MESH_IDS)
+    pl.semaphore_signal(barrier, inc=1, device_id={"section": other_s}, device_id_type=MESH_IDS)
+    pl.semaphore_signal(barrier, inc=1, device_id={"groups": other_g}, device_id_type=MESH_IDS)
+
+    own_copy = pltpu.make_async_copy(latent_ref.at[0, :, lanes(t)], xin.at[t], own_sem)
+    own_copy.start()
+    mod_copy = pltpu.make_async_copy(modulation_ref.at[0, :, lanes(t)], mods.at[s], mod_sem)
+    mod_copy.start()
+    local = []
+    for j in range(heads):
+        copy = pltpu.make_async_copy(
+            weights_ref.at[0, :, t * heads + j], held.at[s, :, j], local_sem.at[j]
+        )
+        copy.start()
+        local.append(copy)
+
+    row = lax.broadcasted_iota(jnp.int32, (rows, tokens), 0)
+    key = lax.broadcasted_iota(jnp.int32, (rows, tokens), 1)
+    tile_rows = rows // tiles
+    row_tile = row // tile_rows
+    key_tile = key % rows // tile_rows
+    distance = t - key // rows
+    column = (span - 1 - distance) * tiles + key_tile
+    marked = jnp.zeros((rows, tokens), jnp.int32)
+    for a in range(tiles):
+        for c in range(columns):
+            marked = jnp.where((row_tile == a) & (column == c), marks_ref[0, a, c], marked)
+    own_tile = (distance == 0) & (row_tile == key_tile)
+    seen = (distance >= 0) & (distance < window_ref[s]) & (own_tile | (marked == 1))
+    marks[t] = jnp.where(seen, 1.0, 0.0).astype(jnp.bfloat16)
+
+    pl.semaphore_wait(barrier, len(peers) + 2)
+
+    half = pl.ds(2 * g, 2)
+    other_half = pl.ds(2 * other_g, 2)
+    mod_remote = remote(
+        modulation_ref.at[0, :, lanes(t)], mods.at[s], modx_sem.at[0], modx_sem.at[1], section=other_s
+    )
+    x_copies = [
+        remote(
+            weights_ref.at[0, half, t * heads + j], held.at[s, half, j],
+            x_send.at[j], x_recv.at[j], section=other_s,
+        )
+        for j in range(heads)
+    ]
+    y_copies = [
+        remote(
+            held.at[other_s, half, j], held.at[other_s, half, j],
+            y_send.at[j], y_recv.at[j], groups=other_g,
+        )
+        for j in range(heads)
+    ]
+    in_copies, mark_copies = [], []
+    for dt in range(1, stretches):
+        pt = lax.rem(t + dt, stretches)
+        in_copies.append(
+            remote(latent_ref.at[0, :, lanes(pt)], xin.at[t], in_send.at[dt], in_recv.at[dt], tm=pt)
+        )
+        mark_copies.append(
+            remote(marks.at[t], marks.at[t], mark_send.at[dt], mark_recv.at[dt], tm=pt)
+        )
+    x_copies[0].start()
+    for copy in in_copies:
+        copy.start()
+    mod_remote.start()
+    for copy in x_copies[1:]:
+        copy.start()
+    for copy in mark_copies:
+        copy.start()
+
+    def forward(j):
+        remote(
+            weights_ref.at[0, half, t * heads + j], held.at[other_s, half, j],
+            x_send.at[j], x_recv.at[j], section=other_s,
+        ).wait_recv()
+        y_copies[j].start()
+
+    def wait_forwarded(j):
+        remote(
+            held.at[other_s, half, j], held.at[other_s, other_half, j],
+            y_send.at[j], y_recv.at[j], groups=other_g,
+        ).wait_recv()
+
+    slot = t * cores + h
+
+    def square_copies(layer):
+        return [
+            remote(
+                squares.at[layer, slot], squares.at[layer, slot],
+                sq_send.at[layer, dt * cores + dh], sq_recv.at[layer, dt * cores + dh],
+                tm=pt, head=ph,
+            )
+            for dt, dh, pt, ph in peers
+        ]
+
+    def share_squares(layer, total):
+        turned = total.T
+        squares[layer, slot] = jnp.sum(turned.reshape(size // 8, 8, tokens), axis=0)
+        for copy in square_copies(layer):
+            copy.start()
+
+    def row_scale(layer):
+        for dt, dh, pt, ph in peers:
+            st = lax.rem(t - dt + stretches, stretches)
+            sh = lax.rem(h - dh + cores, cores)
+            source = st * cores + sh
+            remote(
+                squares.at[layer, slot], squares.at[layer, source],
+                sq_send.at[layer, dt * cores + dh], sq_recv.at[layer, dt * cores + dh],
+                tm=pt, head=ph,
+            ).wait_recv()
+        total = jnp.sum(jnp.sum(squares[layer], axis=0), axis=0, keepdims=True)
+        inverse = lax.rsqrt(total / D + epsilon)
+        return jnp.broadcast_to(inverse, (size, tokens)).T
+
+    def block_of(ref, j):
+        return ref[:, :, j * size : (j + 1) * size].reshape(tokens, size)
+
+    def one_head(layer, j, values, inverse, allowed):
+        modulate = mods[layer, :, j * size : (j + 1) * size]
+        normed = (values * inverse * (1.0 + modulate[1:2]) + modulate[0:1]).astype(jnp.bfloat16)
+        q, k, v = (
+            jnp.dot(normed, held[layer, m, j], preferred_element_type=jnp.float32).astype(jnp.bfloat16)
+            for m in range(3)
+        )
+        scores = lax.dot_general(
+            q, k, (((1,), (1,)), ((), ())), preferred_element_type=jnp.float32
+        ) * scale
+        scores = jnp.where(allowed, scores, -1e30)
+        weight = jnp.exp(scores - jnp.max(scores, axis=-1, keepdims=True))
+        probs = (weight / jnp.sum(weight, axis=-1, keepdims=True)).astype(jnp.bfloat16)
+        attended = jnp.dot(probs, v, preferred_element_type=jnp.float32).astype(jnp.bfloat16)
+        mixed = jnp.dot(attended, held[layer, 3, j], preferred_element_type=jnp.float32)
+        return (values + modulate[2:3] * mixed).astype(jnp.bfloat16)
+
+    own_copy.wait()
+    for dt in range(1, stretches):
+        st = lax.rem(t - dt + stretches, stretches)
+        remote(
+            latent_ref.at[0, :, lanes(t)], xin.at[st], in_send.at[dt], in_recv.at[dt], tm=st
+        ).wait_recv()
+    total = jnp.zeros((tokens, size), jnp.float32)
+    for j in range(heads):
+        values = block_of(xin, j).astype(jnp.float32)
+        total += values * values
+    share_squares(0, total)
+
+    for dt in range(1, stretches):
+        st = lax.rem(t - dt + stretches, stretches)
+        remote(marks.at[t], marks.at[st], mark_send.at[dt], mark_recv.at[dt], tm=st).wait_recv()
+    mod_copy.wait()
+    remote(
+        modulation_ref.at[0, :, lanes(t)], mods.at[other_s], modx_sem.at[0], modx_sem.at[1], section=other_s
+    ).wait_recv()
+    allowed = marks[...].reshape(tokens, tokens).astype(jnp.float32) > 0.5
+
+    inverse = row_scale(0)
+    forward(0)
+    total = jnp.zeros((tokens, size), jnp.float32)
+    for j in range(heads):
+        if j + 1 < heads:
+            forward(j + 1)
+
+        @pl.when(s == 0)
+        def _():
+            local[j].wait()
+
+        @pl.when(s == 1)
+        def _():
+            wait_forwarded(j)
+
+        result = one_head(0, j, block_of(xin, j).astype(jnp.float32), inverse, allowed)
+        xmid[j] = result
+        rounded = result.astype(jnp.float32)
+        total += rounded * rounded
+    share_squares(1, total)
+
+    @pl.when(s == 0)
+    def _():
+        for j in range(heads):
+            wait_forwarded(j)
+
+    @pl.when(s == 1)
+    def _():
+        for j in range(heads):
+            local[j].wait()
+
+    inverse = row_scale(1)
+    finals = []
+    for j in range(heads):
+        result = one_head(1, j, xmid[j].astype(jnp.float32), inverse, allowed)
+        stage[j] = result.reshape(stretches, rows, size)
+        place = pl.ds(pl.multiple_of((t * heads + j) * size, size), size)
+        for dt in range(1, stretches):
+            pt = lax.rem(t + dt, stretches)
+            copy = remote(
+                stage.at[j, pt], out_ref.at[0, :, place], out_send.at[j, dt], out_recv.at[j, dt], tm=pt
+            )
+            copy.start()
+            finals.append(copy)
+        copy = pltpu.make_async_copy(stage.at[j, t], out_ref.at[0, :, place], out_own.at[j])
+        copy.start()
+        finals.append(copy)
+
+    for copy in in_copies + mark_copies + [mod_remote] + x_copies + y_copies:
+        copy.wait_send()
+    for layer in range(2):
+        for copy in square_copies(layer):
+            copy.wait_send()
+    for j in range(heads):
+        for dt in range(1, stretches):
+            st = lax.rem(t - dt + stretches, stretches)
+            place = pl.ds(pl.multiple_of((st * heads + j) * size, size), size)
+            remote(
+                stage.at[j, t], out_ref.at[0, :, place], out_send.at[j, dt], out_recv.at[j, dt], tm=st
+            ).wait()
+        pltpu.make_async_copy(
+            stage.at[j, t],
+            out_ref.at[0, :, pl.ds(pl.multiple_of((t * heads + j) * size, size), size)],
+            out_own.at[j],
+        ).wait()
+
+
+def gathered_shards(latent, head_weights, modulation, tile_mask, window):
+    stretches = lax.axis_size("tm")
+    cores = lax.axis_size("head")
+    rows, features = latent.shape[1:]
+    maps, head_count, size = head_weights.shape[1:4]
+    heads = head_count // stretches
+    width = heads * size
+    tokens = stretches * rows
+    partners = stretches * cores
+    dma = pltpu.SemaphoreType.DMA
+    flops = 2 * heads * 6 * 2 * tokens * size * size
+    return pl.pallas_call(
+        functools.partial(rollout_kernel, stretches, cores),
+        out_shape=jax.ShapeDtypeStruct(latent.shape, latent.dtype),
+        in_specs=[pl.BlockSpec(memory_space=pltpu.SMEM)] * 2 + [pl.BlockSpec(memory_space=pl.ANY)] * 3,
+        out_specs=pl.BlockSpec(memory_space=pl.ANY),
+        scratch_shapes=[
+            pltpu.VMEM((stretches, rows, width), jnp.bfloat16),
+            pltpu.VMEM((heads, tokens, size), jnp.bfloat16),
+            pltpu.VMEM((heads, stretches, rows, size), jnp.bfloat16),
+            pltpu.VMEM((stretches, rows, tokens), jnp.bfloat16),
+            pltpu.VMEM((2, maps, heads, size, size), jnp.bfloat16),
+            pltpu.VMEM((2, modulation.shape[1], width), jnp.float32),
+            pltpu.VMEM((2, partners, 8, tokens), jnp.float32),
+            dma((stretches,)), dma((stretches,)), dma((stretches,)), dma((stretches,)),
+            dma, dma, dma((2,)),
+            dma((heads,)), dma((heads,)), dma((heads,)), dma((heads,)), dma((heads,)),
+            dma((2, partners)), dma((2, partners)),
+            dma((heads, stretches)), dma((heads, stretches)), dma((heads,)),
+        ],
+        compiler_params=pltpu.CompilerParams(
+            collective_id=0, has_side_effects=True, vmem_limit_bytes=56 * 2**20
+        ),
+        cost_estimate=pl.CostEstimate(flops=flops, bytes_accessed=4 * 2**20, transcendentals=0),
+    )(tile_mask, window, latent, head_weights, modulation)
+
+
 def solution(mesh):
+    sizes = dict(mesh.shape)
+
+    def shards(latent, head_weights, *rest):
+        pairs = sizes["section"] == 2 and sizes["groups"] == 2 and head_weights.shape[1] == 4
+        even = head_weights.shape[2] % sizes["tm"] == 0
+        chosen = gathered_shards if pairs and even else ring_shards
+        return chosen(latent, head_weights, *rest)
+
     return jax.shard_map(
         shards,
         mesh=mesh,

time: 182 us -> 43.3 us (0.24); the launches traced: 179 us -> 43.1 us
  waiting for transfers between devices: 68 us -> 0 us
  Pallas kernels: 0 us -> 40.1 us
  starting transfers between devices: 39.1 us -> 0 us
  local copies, waits for them, and re-layouts: 38.4 us -> 2.97 us
  matrix products: 17.4 us -> 0 us
  blocking collectives: 9.85 us -> 0 us
  other arithmetic: 5.56 us -> 0 us
    ppermute x12 -> x0, waiting for transfers between devices: 68 us -> none  [the longest x8 48.9 us: from_behind(): return lax.ppermute(block, axis, route)]
    pallas_call x0 -> x1, Pallas kernels: none -> 40.1 us  [gathered_shards(): pl.pallas_call(functools.partial(rollout_kernel, stretches, cores), out_s...]
    ppermute x12 -> x0, starting transfers between devices: 39.1 us -> none  [the longest x8 36.7 us: from_behind(): return lax.ppermute(block, axis, route)]
    dot_general x12 -> x0, matrix products: 17.4 us -> none  [the longest x4 9.87 us: tick_body(): jnp.einsum('qhd,hde->qhe', attended, weights[3], preferred_element_type=j...]
    squeeze x8 -> x0, local copies, waits for them, and re-layouts: 17.1 us -> none  [the longest x4 8.57 us: tick_body(): window_keys[0]]
    psum x4 -> x0, blocking collectives: 9.85 us -> none  [tick_body(): square_sum = lax.psum(jnp.sum(values * values, axis=-1), 'head')]
    while x16 -> x0, local copies, waits for them, and re-layouts: 7.01 us -> none
    slice x4 -> x0, local copies, waits for them, and re-layouts: 4.12 us -> none  [tick_body(): window_keys[0]]
  transfers between devices with their start and end apart: 12 -> 0, of which waited for: 12 -> 0; matrix products, arithmetic and copies ran while one was open for 3% -> 0% of each run, Pallas kernels for 0% -> 0%
where the time goes in v1:
time: 43.3 us; the launch traced here: 43.1 us
  Pallas kernels  40.1 us (93%)
  local copies, waits for them, and re-layouts  2.97 us (7%)
    pallas_call x1, Pallas kernels, gathered_shards(): pl.pallas_call(functools.partial(rollout_kernel, stretches, cores), out_s...  40.1 us
    unnamed x2, local copies, waits for them, and re-layouts  2.97 us

profile of v1, /device:TPU:2, one launch (start us, length us, event | category | flops | bytes accessed | tf_op | source)
XLA Modules:
  0.0 43.1 jit_solution(1682999904033277061)
XLA Ops:
  0.0 1.4 %copy.6.modulation_ref = f32[1,3,2560]{2,1,0:T(4,128)} copy(f32[1,3,2560]{2,0,1:T(1,128)} %param.7) | data formatting | bytes 61440 | tf_op args[2]
  1.4 40.1 %shard_map.55 = bf16[1,32,2560]{2,1,0:T(8,128)(2,1)} custom-call(s32[1,2,6]{2,1,0:T(2,128)} %marks_ref.1, s32[2]{0:T(128)} %window_ref.1, bf16[1,32,2560]{2,1,0:T(8,128)(2,1)} %latent_ref.1, bf16[1,4,20,128,128]{4,3,2,1,0:T(8,128)(2,1)} %weights_ref.1, f32[1,3,2560]{2,1,0:T(4,128)} %copy.6.modulation_ref), custom_call_target="tpu_custom_call" | custom-call | flops 251658240 | bytes 4194304 | tf_op jit(solution)/shard_map/pallas_call | solution.py:378
  41.5 1.6 %copy.8 = bf16[1,32,2560]{2,1,0:T(8,128)(2,1)} copy(bf16[1,32,2560]{2,1,0:T(8,128)(2,1)} %shard_map.55) | data formatting | bytes 327680

commit v2 on v1

--- a/solution.py
+++ b/solution.py
@@ -104,8 +104,8 @@
     stretches, cores,
     marks_ref, window_ref, latent_ref, weights_ref, modulation_ref,
     out_ref,
-    xin, xmid, stage, marks, held, mods, squares,
-    in_send, in_recv, mark_send, mark_recv, own_sem, mod_sem, modx_sem,
+    mine, xin, xmid, stage, marks, held, mods, squares,
+    in_send, in_recv, mark_send, mark_recv, mine_sem, own_sem, mod_sem, modx_sem,
     local_sem, x_send, x_recv, y_send, y_recv,
     sq_send, sq_recv, out_send, out_recv, out_own,
 ):
@@ -145,9 +145,11 @@
     pl.semaphore_signal(barrier, inc=1, device_id={"section": other_s}, device_id_type=MESH_IDS)
     pl.semaphore_signal(barrier, inc=1, device_id={"groups": other_g}, device_id_type=MESH_IDS)
 
+    mine_copy = pltpu.make_async_copy(latent_ref.at[0], mine, mine_sem)
+    mine_copy.start()
     own_copy = pltpu.make_async_copy(latent_ref.at[0, :, lanes(t)], xin.at[t], own_sem)
     own_copy.start()
-    mod_copy = pltpu.make_async_copy(modulation_ref.at[0, :, lanes(t)], mods.at[s], mod_sem)
+    mod_copy = pltpu.make_async_copy(modulation_ref.at[:, :, lanes(t)], mods.at[s], mod_sem)
     mod_copy.start()
     local = []
     for j in range(heads):
@@ -172,58 +174,6 @@
     seen = (distance >= 0) & (distance < window_ref[s]) & (own_tile | (marked == 1))
     marks[t] = jnp.where(seen, 1.0, 0.0).astype(jnp.bfloat16)
 
-    pl.semaphore_wait(barrier, len(peers) + 2)
-
-    half = pl.ds(2 * g, 2)
-    other_half = pl.ds(2 * other_g, 2)
-    mod_remote = remote(
-        modulation_ref.at[0, :, lanes(t)], mods.at[s], modx_sem.at[0], modx_sem.at[1], section=other_s
-    )
-    x_copies = [
-        remote(
-            weights_ref.at[0, half, t * heads + j], held.at[s, half, j],
-            x_send.at[j], x_recv.at[j], section=other_s,
-        )
-        for j in range(heads)
-    ]
-    y_copies = [
-        remote(
-            held.at[other_s, half, j], held.at[other_s, half, j],
-            y_send.at[j], y_recv.at[j], groups=other_g,
-        )
-        for j in range(heads)
-    ]
-    in_copies, mark_copies = [], []
-    for dt in range(1, stretches):
-        pt = lax.rem(t + dt, stretches)
-        in_copies.append(
-            remote(latent_ref.at[0, :, lanes(pt)], xin.at[t], in_send.at[dt], in_recv.at[dt], tm=pt)
-        )
-        mark_copies.append(
-            remote(marks.at[t], marks.at[t], mark_send.at[dt], mark_recv.at[dt], tm=pt)
-        )
-    x_copies[0].start()
-    for copy in in_copies:
-        copy.start()
-    mod_remote.start()
-    for copy in x_copies[1:]:
-        copy.start()
-    for copy in mark_copies:
-        copy.start()
-
-    def forward(j):
-        remote(
-            weights_ref.at[0, half, t * heads + j], held.at[other_s, half, j],
-            x_send.at[j], x_recv.at[j], section=other_s,
-        ).wait_recv()
-        y_copies[j].start()
-
-    def wait_forwarded(j):
-        remote(
-            held.at[other_s, half, j], held.at[other_s, other_half, j],
-            y_send.at[j], y_recv.at[j], groups=other_g,
-        ).wait_recv()
-
     slot = t * cores + h
 
     def square_copies(layer):
@@ -236,11 +186,65 @@
             for dt, dh, pt, ph in peers
         ]
 
-    def share_squares(layer, total):
+    def put_squares(layer, total):
         turned = total.T
         squares[layer, slot] = jnp.sum(turned.reshape(size // 8, 8, tokens), axis=0)
-        for copy in square_copies(layer):
-            copy.start()
+
+    mine_copy.wait()
+    total = jnp.zeros((rows, size), jnp.float32)
+    for j in range(stretches * heads):
+        values = mine[:, j * size : (j + 1) * size].astype(jnp.float32)
+        total += values * values
+    put_squares(0, jnp.concatenate([total] * stretches, axis=0))
+
+    pl.semaphore_wait(barrier, len(peers) + 2)
+
+    half = pl.ds(2 * g, 2)
+    other_half = pl.ds(2 * other_g, 2)
+    mod_remote = remote(
+        modulation_ref.at[:, :, lanes(t)], mods.at[s], modx_sem.at[0], modx_sem.at[1], section=other_s
+    )
+    x_copies = [
+        remote(
+            weights_ref.at[0, half, t * heads + j], held.at[s, half, j],
+            x_send.at[j], x_recv.at[j], section=other_s,
+        )
+        for j in range(heads)
+    ]
+    y_copies = [
+        remote(
+            held.at[other_s, half, j], held.at[other_s, half, j],
+            y_send.at[j], y_recv.at[j], groups=other_g,
+        )
+        for j in range(heads)
+    ]
+    in_copies, mark_copies = [], []
+    for dt in range(1, stretches):
+        pt = lax.rem(t + dt, stretches)
+        in_copies.append(
+            remote(latent_ref.at[0, :, lanes(pt)], xin.at[t], in_send.at[dt], in_recv.at[dt], tm=pt)
+        )
+        mark_copies.append(
+            remote(marks.at[t], marks.at[t], mark_send.at[dt], mark_recv.at[dt], tm=pt)
+        )
+    first_squares = square_copies(0)
+    for copy in x_copies[:2] + in_copies + first_squares + x_copies[2:] + [mod_remote]:
+        copy.start()
+    for copy in mark_copies:
+        copy.start()
+
+    def forward(j):
+        remote(
+            weights_ref.at[0, half, t * heads + j], held.at[other_s, half, j],
+            x_send.at[j], x_recv.at[j], section=other_s,
+        ).wait_recv()
+        y_copies[j].start()
+
+    def wait_forwarded(j):
+        remote(
+            held.at[other_s, half, j], held.at[other_s, other_half, j],
+            y_send.at[j], y_recv.at[j], groups=other_g,
+        ).wait_recv()
 
     def row_scale(layer):
         for dt, dh, pt, ph in peers:
@@ -252,57 +256,80 @@
                 sq_send.at[layer, dt * cores + dh], sq_recv.at[layer, dt * cores + dh],
                 tm=pt, head=ph,
             ).wait_recv()
-        total = jnp.sum(jnp.sum(squares[layer], axis=0), axis=0, keepdims=True)
+        if layer == 0:
+            stretch = lax.broadcasted_iota(jnp.int32, (8, tokens), 1) // rows
+            total = jnp.zeros((8, tokens), jnp.float32)
+            for source in range(stretches * cores):
+                total += jnp.where(stretch == source // cores, squares[0, source], 0.0)
+        else:
+            total = jnp.sum(squares[layer], axis=0)
+        total = jnp.sum(total, axis=0, keepdims=True)
         inverse = lax.rsqrt(total / D + epsilon)
         return jnp.broadcast_to(inverse, (size, tokens)).T
 
     def block_of(ref, j):
         return ref[:, :, j * size : (j + 1) * size].reshape(tokens, size)
 
-    def one_head(layer, j, values, inverse, allowed):
-        modulate = mods[layer, :, j * size : (j + 1) * size]
-        normed = (values * inverse * (1.0 + modulate[1:2]) + modulate[0:1]).astype(jnp.bfloat16)
+    def some_heads(layer, numbers, inputs, inverse, allowed):
+        modulate = [mods[layer, :, 0, j * size : (j + 1) * size] for j in numbers]
+        normed = [
+            (x * inverse * (1.0 + m[1:2]) + m[0:1]).astype(jnp.bfloat16)
+            for x, m in zip(inputs, modulate)
+        ]
         q, k, v = (
-            jnp.dot(normed, held[layer, m, j], preferred_element_type=jnp.float32).astype(jnp.bfloat16)
+            [
+                jnp.dot(n, held[layer, m, j], preferred_element_type=jnp.float32).astype(jnp.bfloat16)
+                for j, n in zip(numbers, normed)
+            ]
             for m in range(3)
         )
-        scores = lax.dot_general(
-            q, k, (((1,), (1,)), ((), ())), preferred_element_type=jnp.float32
-        ) * scale
-        scores = jnp.where(allowed, scores, -1e30)
-        weight = jnp.exp(scores - jnp.max(scores, axis=-1, keepdims=True))
-        probs = (weight / jnp.sum(weight, axis=-1, keepdims=True)).astype(jnp.bfloat16)
-        attended = jnp.dot(probs, v, preferred_element_type=jnp.float32).astype(jnp.bfloat16)
-        mixed = jnp.dot(attended, held[layer, 3, j], preferred_element_type=jnp.float32)
-        return (values + modulate[2:3] * mixed).astype(jnp.bfloat16)
-
+        scores = [
+            lax.dot_general(a, b, (((1,), (1,)), ((), ())), preferred_element_type=jnp.float32) * scale
+            for a, b in zip(q, k)
+        ]
+        scores = [jnp.where(allowed, x, -1e30) for x in scores]
+        weight = [jnp.exp(x - jnp.max(x, axis=-1, keepdims=True)) for x in scores]
+        probs = [(x / jnp.sum(x, axis=-1, keepdims=True)).astype(jnp.bfloat16) for x in weight]
+        attended = [
+            jnp.dot(p, b, preferred_element_type=jnp.float32).astype(jnp.bfloat16)
+            for p, b in zip(probs, v)
+        ]
+        mixed = [
+            jnp.dot(a, held[layer, 3, j], preferred_element_type=jnp.float32)
+            for j, a in zip(numbers, attended)
+        ]
+        return [
+            (x + m[2:3] * y).astype(jnp.bfloat16) for x, m, y in zip(inputs, modulate, mixed)
+        ]
+
+    def ahead(j):
+        if j < heads:
+            forward(j)
+
+    ahead(0)
+    ahead(1)
     own_copy.wait()
     for dt in range(1, stretches):
         st = lax.rem(t - dt + stretches, stretches)
         remote(
             latent_ref.at[0, :, lanes(t)], xin.at[st], in_send.at[dt], in_recv.at[dt], tm=st
         ).wait_recv()
-    total = jnp.zeros((tokens, size), jnp.float32)
-    for j in range(heads):
-        values = block_of(xin, j).astype(jnp.float32)
-        total += values * values
-    share_squares(0, total)
+    ahead(2)
 
     for dt in range(1, stretches):
         st = lax.rem(t - dt + stretches, stretches)
         remote(marks.at[t], marks.at[st], mark_send.at[dt], mark_recv.at[dt], tm=st).wait_recv()
     mod_copy.wait()
     remote(
-        modulation_ref.at[0, :, lanes(t)], mods.at[other_s], modx_sem.at[0], modx_sem.at[1], section=other_s
+        modulation_ref.at[:, :, lanes(t)], mods.at[other_s], modx_sem.at[0], modx_sem.at[1], section=other_s
     ).wait_recv()
     allowed = marks[...].reshape(tokens, tokens).astype(jnp.float32) > 0.5
 
     inverse = row_scale(0)
-    forward(0)
+    ahead(3)
     total = jnp.zeros((tokens, size), jnp.float32)
     for j in range(heads):
-        if j + 1 < heads:
-            forward(j + 1)
+        ahead(j + 4)
 
         @pl.when(s == 0)
         def _():
@@ -312,11 +339,13 @@
         def _():
             wait_forwarded(j)
 
-        result = one_head(0, j, block_of(xin, j).astype(jnp.float32), inverse, allowed)
+        (result,) = some_heads(0, [j], [block_of(xin, j).astype(jnp.float32)], inverse, allowed)
         xmid[j] = result
         rounded = result.astype(jnp.float32)
         total += rounded * rounded
-    share_squares(1, total)
+    put_squares(1, total)
+    for copy in square_copies(1):
+        copy.start()
 
     @pl.when(s == 0)
     def _():
@@ -330,8 +359,9 @@
 
     inverse = row_scale(1)
     finals = []
-    for j in range(heads):
-        result = one_head(1, j, xmid[j].astype(jnp.float32), inverse, allowed)
+    numbers = list(range(heads))
+    inputs = [xmid[j].astype(jnp.float32) for j in numbers]
+    for j, result in enumerate(some_heads(1, numbers, inputs, inverse, allowed)):
         stage[j] = result.reshape(stretches, rows, size)
         place = pl.ds(pl.multiple_of((t * heads + j) * size, size), size)
         for dt in range(1, stretches):
@@ -381,15 +411,16 @@
         in_specs=[pl.BlockSpec(memory_space=pltpu.SMEM)] * 2 + [pl.BlockSpec(memory_space=pl.ANY)] * 3,
         out_specs=pl.BlockSpec(memory_space=pl.ANY),
         scratch_shapes=[
+            pltpu.VMEM((rows, features), jnp.bfloat16),
             pltpu.VMEM((stretches, rows, width), jnp.bfloat16),
             pltpu.VMEM((heads, tokens, size), jnp.bfloat16),
             pltpu.VMEM((heads, stretches, rows, size), jnp.bfloat16),
             pltpu.VMEM((stretches, rows, tokens), jnp.bfloat16),
             pltpu.VMEM((2, maps, heads, size, size), jnp.bfloat16),
-            pltpu.VMEM((2, modulation.shape[1], width), jnp.float32),
+            pltpu.VMEM((2, modulation.shape[1], 1, width), jnp.float32),
             pltpu.VMEM((2, partners, 8, tokens), jnp.float32),
             dma((stretches,)), dma((stretches,)), dma((stretches,)), dma((stretches,)),
-            dma, dma, dma((2,)),
+            dma, dma, dma, dma((2,)),
             dma((heads,)), dma((heads,)), dma((heads,)), dma((heads,)), dma((heads,)),
             dma((2, partners)), dma((2, partners)),
             dma((heads, stretches)), dma((heads, stretches)), dma((heads,)),
@@ -398,7 +429,7 @@
             collective_id=0, has_side_effects=True, vmem_limit_bytes=56 * 2**20
         ),
         cost_estimate=pl.CostEstimate(flops=flops, bytes_accessed=4 * 2**20, transcendentals=0),
-    )(tile_mask, window, latent, head_weights, modulation)
+    )(tile_mask, window, latent, head_weights, jnp.swapaxes(modulation, 0, 1))
 
 
 def solution(mesh):

time: 43.3 us -> 32.3 us (0.75)
  Pallas kernels: 40.1 us -> 30.1 us
  local copies, waits for them, and re-layouts: 2.97 us -> 1.59 us
    pallas_call x1, Pallas kernels: 40.1 us -> 30.1 us  [gathered_shards(): pl.pallas_call(functools.partial(rollout_kernel, stretches, cores), out_s...]
    unnamed x2 -> x1, local copies, waits for them, and re-layouts: 2.97 us -> 1.59 us
where the time goes in v2:
time: 32.3 us; the launch traced here: 31.7 us
  Pallas kernels  30.1 us (93%)
  local copies, waits for them, and re-layouts  1.59 us (5%)
    pallas_call x1, Pallas kernels, gathered_shards(): pl.pallas_call(functools.partial(rollout_kernel, stretches, cores), out_s...  30.1 us
    unnamed x1, local copies, waits for them, and re-layouts  1.59 us

profile of v2, /device:TPU:2, one launch (start us, length us, event | category | flops | bytes accessed | tf_op | source)
XLA Modules:
  0.0 31.7 jit_solution(6993256619155223519)
XLA Ops:
  0.0 30.1 %shard_map.55 = bf16[1,32,2560]{2,1,0:T(8,128)(2,1)} custom-call(s32[1,2,6]{2,1,0:T(2,128)} %marks_ref.1, s32[2]{0:T(128)} %window_ref.1, bf16[1,32,2560]{2,1,0:T(8,128)(2,1)} %latent_ref.1, bf16[1,4,20,128,128]{4,3,2,1,0:T(8,128)(2,1)} %weights_ref.1, f32[3,1,2560]{2,1,0:T(1,128)} %bitcast.1), custom_call_target="tpu_custom_call" | custom-call | flops 251658240 | bytes 4194304 | tf_op jit(solution)/shard_map/pallas_call | solution.py:408
  30.1 1.6 %copy.7 = bf16[1,32,2560]{2,1,0:T(8,128)(2,1)} copy(bf16[1,32,2560]{2,1,0:T(8,128)(2,1)} %shard_map.55) | data formatting | bytes 327680

commit v3 on v2

--- a/solution.py
+++ b/solution.py
@@ -328,21 +328,25 @@
     inverse = row_scale(0)
     ahead(3)
     total = jnp.zeros((tokens, size), jnp.float32)
-    for j in range(heads):
-        ahead(j + 4)
+    for group in (range(heads // 2), range(heads // 2, heads)):
+        for j in group:
+            ahead(j + 4)
 
         @pl.when(s == 0)
         def _():
-            local[j].wait()
+            for j in group:
+                local[j].wait()
 
         @pl.when(s == 1)
         def _():
-            wait_forwarded(j)
-
-        (result,) = some_heads(0, [j], [block_of(xin, j).astype(jnp.float32)], inverse, allowed)
-        xmid[j] = result
-        rounded = result.astype(jnp.float32)
-        total += rounded * rounded
+            for j in group:
+                wait_forwarded(j)
+
+        inputs = [block_of(xin, j).astype(jnp.float32) for j in group]
+        for j, result in zip(group, some_heads(0, group, inputs, inverse, allowed)):
+            xmid[j] = result
+            rounded = result.astype(jnp.float32)
+            total += rounded * rounded
     put_squares(1, total)
     for copy in square_copies(1):
         copy.start()
@@ -358,40 +362,33 @@
             local[j].wait()
 
     inverse = row_scale(1)
-    finals = []
     numbers = list(range(heads))
     inputs = [xmid[j].astype(jnp.float32) for j in numbers]
     for j, result in enumerate(some_heads(1, numbers, inputs, inverse, allowed)):
-        stage[j] = result.reshape(stretches, rows, size)
-        place = pl.ds(pl.multiple_of((t * heads + j) * size, size), size)
-        for dt in range(1, stretches):
-            pt = lax.rem(t + dt, stretches)
-            copy = remote(
-                stage.at[j, pt], out_ref.at[0, :, place], out_send.at[j, dt], out_recv.at[j, dt], tm=pt
-            )
-            copy.start()
-            finals.append(copy)
-        copy = pltpu.make_async_copy(stage.at[j, t], out_ref.at[0, :, place], out_own.at[j])
+        stage[:, :, j * size : (j + 1) * size] = result.reshape(stretches, rows, size)
+    finals = []
+    for dt in range(1, stretches):
+        pt = lax.rem(t + dt, stretches)
+        copy = remote(
+            stage.at[pt], out_ref.at[0, :, lanes(t)], out_send.at[0, dt], out_recv.at[0, dt], tm=pt
+        )
         copy.start()
         finals.append(copy)
+    last = pltpu.make_async_copy(stage.at[t], out_ref.at[0, :, lanes(t)], out_own.at[0])
+    last.start()
 
     for copy in in_copies + mark_copies + [mod_remote] + x_copies + y_copies:
         copy.wait_send()
     for layer in range(2):
         for copy in square_copies(layer):
             copy.wait_send()
-    for j in range(heads):
-        for dt in range(1, stretches):
-            st = lax.rem(t - dt + stretches, stretches)
-            place = pl.ds(pl.multiple_of((st * heads + j) * size, size), size)
-            remote(
-                stage.at[j, t], out_ref.at[0, :, place], out_send.at[j, dt], out_recv.at[j, dt], tm=st
-            ).wait()
-        pltpu.make_async_copy(
-            stage.at[j, t],
-            out_ref.at[0, :, pl.ds(pl.multiple_of((t * heads + j) * size, size), size)],
-            out_own.at[j],
-        ).wait()
+    for dt in range(1, stretches):
+        st = lax.rem(t - dt + stretches, stretches)
+        finals[dt - 1].wait_send()
+        remote(
+            stage.at[t], out_ref.at[0, :, lanes(st)], out_send.at[0, dt], out_recv.at[0, dt], tm=st
+        ).wait_recv()
+    last.wait()
 
 
 def gathered_shards(latent, head_weights, modulation, tile_mask, window):
@@ -414,7 +411,7 @@
             pltpu.VMEM((rows, features), jnp.bfloat16),
             pltpu.VMEM((stretches, rows, width), jnp.bfloat16),
             pltpu.VMEM((heads, tokens, size), jnp.bfloat16),
-            pltpu.VMEM((heads, stretches, rows, size), jnp.bfloat16),
+            pltpu.VMEM((stretches, rows, width), jnp.bfloat16),
             pltpu.VMEM((stretches, rows, tokens), jnp.bfloat16),
             pltpu.VMEM((2, maps, heads, size, size), jnp.bfloat16),
             pltpu.VMEM((2, modulation.shape[1], 1, width), jnp.float32),

time: 32.3 us -> 31.4 us (0.972); the launches traced: 31.7 us -> 31.3 us
  Pallas kernels: 30.1 us -> 29.7 us
    pallas_call x1, Pallas kernels: 30.1 us -> 29.7 us  [gathered_shards(): pl.pallas_call(functools.partial(rollout_kernel, stretches, cores), out_s...]
where the time goes in v3:
time: 31.4 us; the launch traced here: 31.3 us
  Pallas kernels  29.7 us (95%)
  local copies, waits for them, and re-layouts  1.59 us (5%)
    pallas_call x1, Pallas kernels, gathered_shards(): pl.pallas_call(functools.partial(rollout_kernel, stretches, cores), out_s...  29.7 us
    unnamed x1, local copies, waits for them, and re-layouts  1.59 us

profile of v3, /device:TPU:2, one launch (start us, length us, event | category | flops | bytes accessed | tf_op | source)
XLA Modules:
  0.0 31.3 jit_solution(13664929739768011392)
XLA Ops:
  0.0 29.7 %shard_map.55 = bf16[1,32,2560]{2,1,0:T(8,128)(2,1)} custom-call(s32[1,2,6]{2,1,0:T(2,128)} %marks_ref.1, s32[2]{0:T(128)} %window_ref.1, bf16[1,32,2560]{2,1,0:T(8,128)(2,1)} %latent_ref.1, bf16[1,4,20,128,128]{4,3,2,1,0:T(8,128)(2,1)} %weights_ref.1, f32[3,1,2560]{2,1,0:T(1,128)} %bitcast.1), custom_call_target="tpu_custom_call" | custom-call | flops 251658240 | bytes 4194304 | tf_op jit(solution)/shard_map/pallas_call | solution.py:405
  29.7 1.6 %copy.7 = bf16[1,32,2560]{2,1,0:T(8,128)(2,1)} copy(bf16[1,32,2560]{2,1,0:T(8,128)(2,1)} %shard_map.55) | data formatting | bytes 327680

commit v4 on v3

--- a/solution.py
+++ b/solution.py
@@ -228,7 +228,7 @@
             remote(marks.at[t], marks.at[t], mark_send.at[dt], mark_recv.at[dt], tm=pt)
         )
     first_squares = square_copies(0)
-    for copy in x_copies[:2] + in_copies + first_squares + x_copies[2:] + [mod_remote]:
+    for copy in x_copies + in_copies[::-1] + first_squares[::-1] + [mod_remote]:
         copy.start()
     for copy in mark_copies:
         copy.start()
@@ -315,6 +315,9 @@
             latent_ref.at[0, :, lanes(t)], xin.at[st], in_send.at[dt], in_recv.at[dt], tm=st
         ).wait_recv()
     ahead(2)
+    ahead(3)
+    for j in range(4, heads):
+        ahead(j)
 
     for dt in range(1, stretches):
         st = lax.rem(t - dt + stretches, stretches)
@@ -326,12 +329,8 @@
     allowed = marks[...].reshape(tokens, tokens).astype(jnp.float32) > 0.5
 
     inverse = row_scale(0)
-    ahead(3)
     total = jnp.zeros((tokens, size), jnp.float32)
     for group in (range(heads // 2), range(heads // 2, heads)):
-        for j in group:
-            ahead(j + 4)
-
         @pl.when(s == 0)
         def _():
             for j in group:
@@ -348,7 +347,7 @@
             rounded = result.astype(jnp.float32)
             total += rounded * rounded
     put_squares(1, total)
-    for copy in square_copies(1):
+    for copy in square_copies(1)[::-1]:
         copy.start()
 
     @pl.when(s == 0)

time: 31.4 us -> 30.4 us (0.968)
  Pallas kernels: 29.7 us -> 28.6 us
    pallas_call x1, Pallas kernels: 29.7 us -> 28.6 us  [gathered_shards(): pl.pallas_call(functools.partial(rollout_kernel, stretches, cores), out_s...]
where the time goes in v4:
time: 30.4 us; the launch traced here: 30.2 us
  Pallas kernels  28.6 us (94%)
  local copies, waits for them, and re-layouts  1.59 us (5%)
    pallas_call x1, Pallas kernels, gathered_shards(): pl.pallas_call(functools.partial(rollout_kernel, stretches, cores), out_s...  28.6 us
    unnamed x1, local copies, waits for them, and re-layouts  1.59 us

profile of v4, /device:TPU:2, one launch (start us, length us, event | category | flops | bytes accessed | tf_op | source)
XLA Modules:
  0.0 30.2 jit_solution(10101393190635239124)
XLA Ops:
  0.0 28.6 %shard_map.55 = bf16[1,32,2560]{2,1,0:T(8,128)(2,1)} custom-call(s32[1,2,6]{2,1,0:T(2,128)} %marks_ref.1, s32[2]{0:T(128)} %window_ref.1, bf16[1,32,2560]{2,1,0:T(8,128)(2,1)} %latent_ref.1, bf16[1,4,20,128,128]{4,3,2,1,0:T(8,128)(2,1)} %weights_ref.1, f32[3,1,2560]{2,1,0:T(1,128)} %bitcast.1), custom_call_target="tpu_custom_call" | custom-call | flops 251658240 | bytes 4194304 | tf_op jit(solution)/shard_map/pallas_call | solution.py:404
  28.6 1.6 %copy.7 = bf16[1,32,2560]{2,1,0:T(8,128)(2,1)} copy(bf16[1,32,2560]{2,1,0:T(8,128)(2,1)} %shard_map.55) | data formatting | bytes 327680
